TPU v7x, 32 devices: a whole 2x2x4 slice. The times are simulated.
32 devices in a mesh: dp: 8 (over z, x), mp: 4 (over y, core).
Axes of the slice: x: 2, y: 2, z: 4, core: 2. Of those that a mesh axis runs over, the one named last changes fastest.
Arguments:
- embed_table: float32 [16, 4096, 256], P('mp', 'dp'), may hold values from -5 to 5
- accum: float32 [16, 4096], P('mp', 'dp'), may hold values from 0.1 to 3
- stale_grad: bfloat16 [16, 4096, 256], P('mp', 'dp'), may hold values from -6 to 6
- grad_owner: int32 [16, 4096, 1], P('mp', 'dp'), may hold values from 0 to 7; in each aligned block of 512 rows (0 to 511, 512 to 1023, ..., all dimensions but the last counted through in order) at most 128 rows name the same one
- grad_row: int32 [16, 4096], P('mp', 'dp'), may hold values from 0 to 511
- lookup_owner: int32 [16, 4096, 1], P('mp', 'dp'), may hold values from 0 to 7; in each aligned block of 512 rows (0 to 511, 512 to 1023, ..., all dimensions but the last counted through in order) at most 128 rows name the same one
- lookup_row: int32 [16, 4096], P('mp', 'dp'), may hold values from 0 to 511
- bag_len: int32 [16, 2048], P('mp', 'dp'), may hold values from 1 to 2
- label: int32 [2048], P('dp'), may hold values 0 or 1
- up_factor_weight: bfloat16 [2, 512, 4096], P(None, None, 'mp'), may hold values from -0.25 to 0.25
- v_weight: bfloat16 [2, 512, 4096], P(None, None, 'mp'), may hold values from -0.09375 to 0.09375
- cross_bias: float32 [2, 4096], P(None, 'mp'), may hold values from -3 to 3
- head_weight: float32 [4096], P('mp'), may hold values from -0.09375 to 0.09375
Outputs:
- new_table: float32 [16, 4096, 256], P('mp', 'dp')
- new_accum: float32 [16, 4096], P('mp', 'dp')
- grad_u: float32 [2, 512, 4096], P(None, 'dp', 'mp')
- grad_v: float32 [2, 512, 4096], P(None, 'dp', 'mp')
- grad_small: float32 [3, 4096], P(None, 'mp')
- grad_pooled: bfloat16 [2048, 4096], P('dp', 'mp')
Inputs may be any that keep to these rules, and one draw needn't show every extreme that they name: `grad_owner`: among the 512 blocks of one feature held by one index of dp, at most 128 name the same owner, and in some such group exactly 128 do. `lookup_owner`: among the 512 id slots of one feature belonging to one index of dp, at most 128 name the same owner, and in some such group exactly 128 do; slots k >= bag_len are unused.
All inputs are finite; a program needn't handle non-finite values. No bound on the sum of `label` on one device may be relied on, other than what follows from the above.
Results may differ from a plain program's by a relative error of at most 0.009.
Values may be sent and summed in bfloat16 or wider, within the bound.
A program may use at most 128 MiB of HBM per device.

v0:
```python
import jax
import jax.numpy as jnp
from jax import lax
from jax.sharding import PartitionSpec as P

learn_rate = 0.5


def bucket_slots(owners, capacity, peers):
    count = owners.shape[1]
    onehot = (owners[:, None, :] == jnp.arange(peers)[None, :, None]).astype(jnp.bfloat16)
    earlier = (jnp.arange(count)[:, None] < jnp.arange(count)[None, :]).astype(jnp.bfloat16)
    before = jnp.einsum("fpi,ij->fpj", onehot, earlier, preferred_element_type=jnp.float32)
    order_in = jnp.sum(before * onehot.astype(jnp.float32), axis=1)
    return owners * capacity + order_in.astype(jnp.int32)


def selection_matrix(indices, length):
    return (indices[:, :, None] == jnp.arange(length)[None, None, :]).astype(jnp.bfloat16)


def contract_last(left, right):
    return lax.dot_general(
        left, right, (((1,), (1,)), ((), ())), preferred_element_type=jnp.float32
    )


def contract_first(left, right):
    return lax.dot_general(
        left, right, (((0,), (0,)), ((), ())), preferred_element_type=jnp.float32
    )


def cross_down(state, v_layer):
    return lax.psum(contract_last(state, v_layer), "mp").astype(jnp.bfloat16)


def local(
    embed_table,
    accum,
    stale_grad,
    grad_owner,
    grad_row,
    lookup_owner,
    lookup_row,
    bag_len,
    label,
    up_factor_weight,
    v_weight,
    cross_bias,
    head_weight,
):
    peers = lax.axis_size("dp")
    local_feats, grad_dev, width = stale_grad.shape
    rows_per_shard = embed_table.shape[1]
    which_feature = jnp.arange(local_feats)[:, None]
    grad_cap = max(2, 2 * grad_dev // peers)
    grad_total = peers * grad_cap
    grad_slot = bucket_slots(grad_owner[:, :, 0], grad_cap, peers)
    place = selection_matrix(grad_slot, grad_total)
    send_grads = jnp.einsum(
        "fns,fne->fse", place, stale_grad, preferred_element_type=jnp.float32
    ).astype(jnp.bfloat16)
    send_rows = (
        jnp.full((local_feats, grad_total), rows_per_shard, jnp.int32)
        .at[which_feature, grad_slot]
        .set(grad_row)
    )
    recv_grads = lax.all_to_all(
        send_grads.reshape(local_feats, peers, grad_cap, width),
        "dp",
        split_axis=1,
        concat_axis=1,
        tiled=True,
    )
    recv_rows = lax.all_to_all(
        send_rows.reshape(local_feats, peers, grad_cap),
        "dp",
        split_axis=1,
        concat_axis=1,
        tiled=True,
    )
    landing = selection_matrix(recv_rows.reshape(local_feats, grad_total), rows_per_shard)
    summed = jnp.einsum(
        "wjc,wjl->wcl",
        landing,
        recv_grads.reshape(local_feats, grad_total, width),
        preferred_element_type=jnp.float32,
    )
    new_accum = accum + jnp.mean(summed * summed, axis=2)
    new_table = embed_table - learn_rate * summed / jnp.sqrt(new_accum)[:, :, None]
    batch_dev = bag_len.shape[1]
    look_dev = lookup_row.shape[1]
    bag_size = look_dev // batch_dev
    look_cap = max(2, 2 * look_dev // peers)
    look_total = peers * look_cap
    look_slot = bucket_slots(lookup_owner[:, :, 0], look_cap, peers)
    wanted = (
        jnp.zeros((local_feats, look_total), jnp.int32).at[which_feature, look_slot].set(lookup_row)
    )
    requested_ids = lax.all_to_all(
        wanted.reshape(local_feats, peers, look_cap), "dp", split_axis=1, concat_axis=1, tiled=True
    ).reshape(local_feats, look_total)
    second_table = embed_table.astype(jnp.bfloat16)
    served = jnp.einsum(
        "adv,avm->adm",
        selection_matrix(requested_ids, rows_per_shard),
        second_table,
        preferred_element_type=jnp.float32,
    ).astype(jnp.bfloat16)
    returned = lax.all_to_all(
        served.reshape(local_feats, peers, look_cap, width),
        "dp",
        split_axis=1,
        concat_axis=1,
        tiled=True,
    ).reshape(local_feats, look_total, width)
    slots = look_slot.reshape(local_feats, batch_dev, bag_size)
    mixing = jnp.zeros((local_feats, batch_dev, look_total), jnp.bfloat16)
    for member in range(bag_size):
        used = (bag_len > member).astype(jnp.bfloat16)
        mixing = mixing + selection_matrix(slots[:, :, member], look_total) * used[:, :, None]
    pooled = jnp.einsum(
        "fbs,fse->fbe", mixing, returned, preferred_element_type=jnp.float32
    ).astype(jnp.bfloat16)
    start = jnp.transpose(pooled, (1, 0, 2)).reshape(batch_dev, local_feats * width)
    start_f = start.astype(jnp.float32)
    n_layers = up_factor_weight.shape[0]
    state = start
    states = []
    downs = []
    crosses = []
    for layer in range(n_layers):
        down_sum = cross_down(state, v_weight[layer])
        cross_out = (
            jnp.dot(down_sum, up_factor_weight[layer], preferred_element_type=jnp.float32)
            + cross_bias[layer]
        )
        states.append(state)
        downs.append(down_sum)
        crosses.append(cross_out)
        state = (start_f * cross_out + state.astype(jnp.float32)).astype(jnp.bfloat16)
    logit = lax.psum(jnp.sum(state.astype(jnp.float32) * head_weight[None, :], axis=1), "mp")
    slope = (jax.nn.sigmoid(logit) - label.astype(jnp.float32)) / jnp.sqrt(
        jnp.float32(batch_dev * peers)
    )
    upstream = slope[:, None] * head_weight[None, :]
    head_grad = jnp.sum(slope[:, None] * state.astype(jnp.float32), axis=0)
    to_start = jnp.zeros(start_f.shape, jnp.float32)
    grads_u = [None] * n_layers
    grads_v = [None] * n_layers
    bias_grads = [None] * n_layers
    for layer in reversed(range(n_layers)):
        direct = upstream * start_f
        bias_grads[layer] = jnp.sum(direct, axis=0)
        direct_bias_term = direct.astype(jnp.bfloat16)
        grad_u_layer = contract_first(downs[layer], direct_bias_term)
        back_sum = lax.psum(contract_last(direct_bias_term, up_factor_weight[layer]), "mp").astype(
            jnp.bfloat16
        )
        down_factor_gradient = contract_first(back_sum, states[layer])
        to_start = to_start + upstream * crosses[layer]
        upstream = upstream + jnp.dot(back_sum, v_weight[layer], preferred_element_type=jnp.float32)
        grads_u[layer] = grad_u_layer
        grads_v[layer] = down_factor_gradient
    grad_u = jnp.stack(grads_u)
    grad_v = jnp.stack(grads_v)
    grad_u, grad_v = (
        lax.psum_scatter(grad_u, "dp", scatter_dimension=1, tiled=True),
        lax.psum_scatter(grad_v, "dp", scatter_dimension=1, tiled=True),
    )
    grad_small = lax.psum(jnp.stack(bias_grads + [head_grad]), "dp")
    grad_pooled = (upstream + to_start).astype(jnp.bfloat16)
    return (new_table, new_accum, grad_u, grad_v, grad_small, grad_pooled)


def solution(mesh):
    return jax.shard_map(
        local,
        mesh=mesh,
        in_specs=(
            P("mp", "dp", None),
            P("mp", "dp"),
            P("mp", "dp", None),
            P("mp", "dp", None),
            P("mp", "dp"),
            P("mp", "dp", None),
            P("mp", "dp"),
            P("mp", "dp"),
            P("dp"),
            P(None, None, "mp"),
            P(None, None, "mp"),
            P(None, "mp"),
            P("mp"),
        ),
        out_specs=(
            P("mp", "dp", None),
            P("mp", "dp"),
            P(None, "dp", "mp"),
            P(None, "dp", "mp"),
            P(None, "mp"),
            P("dp", "mp"),
        ),
        check_vma=False,
    )
```

profile of v0, /device:TPU:2, one launch (start us, length us, event | category | flops | bytes accessed | tf_op | source)
XLA Modules:
  0.0 389.2 jit_solution(6501028085515760701)
XLA Ops:
  12.9 8.1 %scatter_custom_fusion.1 = s32[4096]{0:T(1024)S(1)} fusion(s32[2048]{0:T(1024)S(1)} %bitcast.127, s32[2048]{0:T(1024)S(1)} %bitcast.125, s32[]{:T(128)} %constant.5.clone.1), kind=kCustom, calls=%fused_computation.114 | custom fusion | bytes 16388
  20.9 11.2 %all_to_all.20 = s32[4,8,128]{2,0,1:T(4,128)S(1)} all-to-all(s32[4,8,128]{2,0,1:T(4,128)S(1)} %copy.52), channel_id=1, replica_groups=mesh['dp'=8,'mp'=4] {'dp'}, dimensions={1} | all-to-all | bytes 32768 | tf_op jit(solution)/shard_map/all_to_all | solution.py:101
  32.2 3.6 fusion.14
  37.3 5.1 %all-to-all-start.3 = ((bf16[4,8,128,256]{3,2,0,1:T(8,128)(2,1)}), bf16[4,8,128,256]{3,2,0,1:T(8,128)(2,1)S(1)}, u32[]{:S(2)}, u32[]{:S(2)}) async-start(bf16[4,8,128,256]{3,2,0,1:T(8,128)(2,1)} %copy.53), calls=%async_computation.3 | async-start | bytes 4194304 | tf_op jit(solution)/shard_map/all_to_all | solution.py:111
  45.0 44.0 %all-to-all-done.3 = bf16[4,8,128,256]{3,2,0,1:T(8,128)(2,1)S(1)} async-done(((bf16[4,8,128,256]{3,2,0,1:T(8,128)(2,1)}), bf16[4,8,128,256]{3,2,0,1:T(8,128)(2,1)S(1)}, u32[]{:S(2)}, u32[]{:S(2)}) %all-to-all-start.3) | async-done | bytes 2097184 | tf_op jit(solution)/shard_map/all_to_all | solution.py:111
  89.0 2.6 copy.54
  91.5 4.2 %reshape.91 = bf16[4,1024,256]{1,2,0:T(8,128)(2,1)} reshape(bf16[4,8,128,256]{2,1,3,0:T(8,128)(2,1)} %copy.54) | data formatting | bytes 4194304 | tf_op jit(solution)/shard_map/reshape | solution.py:117
  95.7 3.1 fusion.17
  100.7 16.6 %all-reduce.4 = bf16[256,512]{1,0:T(8,128)(2,1)S(1)} all-reduce(f32[256,512]{1,0:T(8,128)S(1)} %fusion.40), channel_id=1, replica_groups=mesh['dp'=8,'mp'=4] {'mp'}, use_global_device_ids=true, to_apply=%region_5.0 | all-reduce | flops 131072 | bytes 786432 | tf_op jit(solution)/shard_map/psum | solution.py:35
  117.4 2.9 fusion.26
  121.5 17.2 %all-reduce.5 = bf16[256,512]{1,0:T(8,128)(2,1)S(1)} all-reduce(f32[256,512]{1,0:T(8,128)} %fusion.34), channel_id=1, replica_groups=mesh['dp'=8,'mp'=4] {'mp'}, use_global_device_ids=true, to_apply=%region_6.0 | all-reduce | flops 131072 | bytes 786432 | tf_op jit(solution)/shard_map/psum | solution.py:35
  138.7 2.9 fusion.23
  141.6 5.7 %psum.44 = f32[256]{0:T(256)S(1)} all-reduce(f32[256]{0:T(256)S(1)} %get-tuple-element.34), channel_id=1, replica_groups=mesh['dp'=8,'mp'=4] {'mp'}, use_global_device_ids=true, to_apply=%region_8.0 | all-reduce | flops 256 | bytes 2048 | tf_op jit(solution)/shard_map/psum | solution.py:143
  147.4 1.9 convolution_bitcast_fusion.2
  150.1 16.9 %all-reduce.6 = bf16[256,512]{1,0:T(8,128)(2,1)} all-reduce(f32[256,512]{1,0:T(8,128)S(1)} %fusion.30), channel_id=1, replica_groups=mesh['dp'=8,'mp'=4] {'mp'}, use_global_device_ids=true, to_apply=%region_9.0 | all-reduce | flops 131072 | bytes 786432 | tf_op jit(solution)/shard_map/psum | solution.py:158
  170.4 2.2 pad_maximum_fusion
  172.8 2.5 fusion.36
  175.2 17.5 %all-reduce.7 = bf16[256,512]{1,0:T(8,128)(2,1)S(1)} all-reduce(f32[256,512]{1,0:T(8,128)} %fusion.36), channel_id=1, replica_groups=mesh['dp'=8,'mp'=4] {'mp'}, use_global_device_ids=true, to_apply=%region_11.0 | all-reduce | flops 131072 | bytes 786432 | tf_op jit(solution)/shard_map/psum | solution.py:158
  194.2 2.3 pad_maximum_fusion.1
  199.5 5.4 %all-to-all-start.1 = ((bf16[4,8,128,256]{3,2,0,1:T(8,128)(2,1)}), bf16[4,8,128,256]{3,2,0,1:T(8,128)(2,1)}, u32[]{:S(2)}, u32[]{:S(2)}) async-start(bf16[4,8,128,256]{3,2,0,1:T(8,128)(2,1)} %copy.45), calls=%async_computation.1 | async-start | bytes 4194304 | tf_op jit(solution)/shard_map/all_to_all | solution.py:69
  204.9 8.1 %scatter_custom_fusion = s32[4096]{0:T(1024)S(1)} fusion(s32[2048]{0:T(1024)S(1)} %bitcast.128, s32[2048]{0:T(1024)S(1)} %bitcast.126, s32[]{:T(128)} %constant.11.clone.1), kind=kCustom, calls=%fused_computation.116 | custom fusion | bytes 16388
  213.6 46.8 %all-to-all-done.1 = bf16[4,8,128,256]{3,2,0,1:T(8,128)(2,1)} async-done(((bf16[4,8,128,256]{3,2,0,1:T(8,128)(2,1)}), bf16[4,8,128,256]{3,2,0,1:T(8,128)(2,1)}, u32[]{:S(2)}, u32[]{:S(2)}) %all-to-all-start.1) | async-done | bytes 2097184 | tf_op jit(solution)/shard_map/all_to_all | solution.py:69
  260.4 4.1 %all-to-all-start = ((s32[4,8,128]{2,0,1:T(4,128)}), s32[4,8,128]{2,0,1:T(4,128)S(1)}, u32[]{:S(2)}, u32[]{:S(2)}) async-start(s32[4,8,128]{2,0,1:T(4,128)} %copy.44), calls=%async_computation | async-start | bytes 32768 | tf_op jit(solution)/shard_map/all_to_all | solution.py:76
  264.5 2.9 copy.47
  267.4 4.4 %copy.46 = bf16[4,8,128,256]{2,1,3,0:T(8,128)(2,1)} copy(bf16[4,8,128,256]{3,2,0,1:T(8,128)(2,1)} %all-to-all-done.1) | data formatting | bytes 4194304 | tf_op jit(solution)/shard_map/all_to_all | solution.py:69
  271.8 4.2 %reshape.88 = bf16[4,1024,256]{1,2,0:T(8,128)(2,1)} reshape(bf16[4,8,128,256]{2,1,3,0:T(8,128)(2,1)} %copy.46) | data formatting | bytes 4194304 | tf_op jit(solution)/shard_map/reshape | solution.py:87
  276.0 4.1 %multiply_reduce_fusion = (f32[4,512]{1,0:T(4,128)S(1)}, f32[4,512,256]{1,2,0:T(8,128)S(1)}) fusion(bf16[4,1024,256]{1,2,0:T(8,128)(2,1)} %reshape.88, s32[4,1024]{1,0:T(4,128)S(1)} %bitcast.120), kind=kOutput, calls=%fused_computation.27 | convolution fusion | flops 1076885504 | bytes 4218880 | tf_op jit(solution)/shard_map/wjc,wjl->wcl/dot_general | solution.py:84
  280.8 1.9 divide_subtract_fusion
  282.7 3.0 copy.56
  286.9 33.2 %psum.47 = f32[3,1024]{1,0:T(4,128)} all-reduce(f32[3,1024]{1,0:T(4,128)S(1)} %pad_maximum_fusion.2), channel_id=1, replica_groups=mesh['dp'=8,'mp'=4] {'dp'}, use_global_device_ids=true, to_apply=%region_16.0 | all-reduce | flops 3072 | bytes 24576 | tf_op jit(solution)/shard_map/psum | solution.py:172
  320.1 2.8 fusion.20
  322.9 59.4 %reduce-scatter.5.cloned.1.call-done = f32[2,64,1024]{2,1,0:T(8,128)} async-done(((f32[2,512,1024]{2,1,0:T(8,128)}), f32[2,64,1024]{2,1,0:T(8,128)}) %reduce-scatter.5.cloned.1.call-update) | async-done | bytes 524304 | tf_op jit(solution)/shard_map/reduce_scatter | solution.py:170
  (81 shorter events, 23.9 us)
Async XLA Ops:
  7.2 189.4 %copy-start = (bf16[4,512,256]{2,1,0:T(8,128)(2,1)S(1)}, bf16[4,512,256]{2,1,0:T(8,128)(2,1)}, u32[]{:S(2)}) copy-start(bf16[4,512,256]{2,1,0:T(8,128)(2,1)} %param.15) | copy-start | bytes 3145732
  37.3 5.3 %copy-start.9 = (f32[1024]{0:T(1024)S(1)}, f32[1024]{0:T(1024)}, u32[]{:S(2)}) copy-start(f32[1024]{0:T(1024)} %param.25) | copy-start | bytes 12292
  37.3 51.7 %all-to-all-start.3 = ((bf16[4,8,128,256]{3,2,0,1:T(8,128)(2,1)}), bf16[4,8,128,256]{3,2,0,1:T(8,128)(2,1)S(1)}, u32[]{:S(2)}, u32[]{:S(2)}) async-start(bf16[4,8,128,256]{3,2,0,1:T(8,128)(2,1)} %copy.53), calls=%async_computation.3 | async-start | bytes 4194304 | tf_op jit(solution)/shard_map/all_to_all | solution.py:111
  42.4 2.5 copy-start.13
  42.4 2.6 copy-start.10
  42.4 280.5 %reduce-scatter.3.cloned.1.call-start = ((), (), s32[]{:S(2)}) async-start(), calls=%async_computation.6 | async-start | bytes 4718592 | tf_op jit(solution)/shard_map/reduce_scatter | solution.py:169
  117.3 2.9 copy-start.8
  120.3 21.3 %copy-start.4 = (bf16[256,1024]{1,0:T(8,128)(2,1)}, bf16[256,1024]{1,0:T(8,128)(2,1)S(1)}, u32[]{:S(2)}) copy-start(bf16[256,1024]{1,0:T(8,128)(2,1)S(1)} %get-tuple-element.52) | copy-start | bytes 1572868
  138.7 8.6 %copy-start.14 = (s32[256]{0:T(256)S(1)}, s32[256]{0:T(256)}, u32[]{:S(2)}) copy-start(s32[256]{0:T(256)} %param.21) | copy-start | bytes 3076
  147.3 2.3 copy-start.3
  168.9 1.6 copy-start.2
  172.7 209.6 %reduce-scatter.5.cloned.1.call-start = ((), (), s32[]{:S(2)}) async-start(), calls=%async_computation.7 | async-start | bytes 4718592 | tf_op jit(solution)/shard_map/reduce_scatter | solution.py:170
  175.2 18.1 %copy-start.5 = (bf16[256,1024]{1,0:T(8,128)(2,1)S(1)}, bf16[256,1024]{1,0:T(8,128)(2,1)}, u32[]{:S(2)}) copy-start(bf16[256,1024]{1,0:T(8,128)(2,1)} %copy-done.4) | copy-start | bytes 1572868
  192.8 1.0 copy-start.7
  199.5 5.4 %copy-start.11 = (s32[4,512]{1,0:T(4,128)S(1)}, s32[4,512]{1,0:T(4,128)}, u32[]{:S(2)}) copy-start(s32[4,512]{1,0:T(4,128)} %param.17) | copy-start | bytes 24580
  199.5 60.9 %all-to-all-start.1 = ((bf16[4,8,128,256]{3,2,0,1:T(8,128)(2,1)}), bf16[4,8,128,256]{3,2,0,1:T(8,128)(2,1)}, u32[]{:S(2)}, u32[]{:S(2)}) async-start(bf16[4,8,128,256]{3,2,0,1:T(8,128)(2,1)} %copy.45), calls=%async_computation.1 | async-start | bytes 4194304 | tf_op jit(solution)/shard_map/all_to_all | solution.py:69
  260.4 15.6 %all-to-all-start = ((s32[4,8,128]{2,0,1:T(4,128)}), s32[4,8,128]{2,0,1:T(4,128)S(1)}, u32[]{:S(2)}, u32[]{:S(2)}) async-start(s32[4,8,128]{2,0,1:T(4,128)} %copy.44), calls=%async_computation | async-start | bytes 32768 | tf_op jit(solution)/shard_map/all_to_all | solution.py:76
  276.0 4.2 %copy-start.12 = (f32[4,512]{1,0:T(4,128)S(1)}, f32[4,512]{1,0:T(4,128)}, u32[]{:S(2)}) copy-start(f32[4,512]{1,0:T(4,128)} %param.14) | copy-start | bytes 24580
  276.0 4.8 %copy-start.1 = (f32[4,512,256]{1,2,0:T(8,128)S(1)}, f32[4,512,256]{1,2,0:T(8,128)}, u32[]{:S(2)}) copy-start(f32[4,512,256]{1,2,0:T(8,128)} %copy.47) | copy-start | bytes 6291460
  282.7 37.4 %copy-start.6 = (f32[256,1024]{1,0:T(8,128)S(1)}, f32[256,1024]{1,0:T(8,128)}, u32[]{:S(2)}) copy-start(f32[256,1024]{1,0:T(8,128)} %get-tuple-element.54) | copy-start | bytes 3145732
Sparse Core Ops, SparseCore 0:
  172.8 116.8 reduce-scatter.2
  294.4 87.9 reduce-scatter.4
where the time goes:
time: 392 us; the launch traced here: 389 us
  waiting for transfers between devices  150 us (38%)
  blocking collectives  118 us (30%)
  local copies, waits for them, and re-layouts  46.2 us (12%)
  matrix products  32.4 us (8%)
  starting transfers between devices  14.7 us (4%)
  between operations  14.4 us (4%)
  other arithmetic  12.8 us (3%)
    reduce_scatter x1, waiting for transfers between devices, local(): lax.psum_scatter(grad_v, 'dp', scatter_dimension=1, tiled=True)  59.4 us
    all_to_all x1, waiting for transfers between devices, local(): lax.all_to_all(send_grads.reshape(local_feats, peers, grad_cap, width), '...  46.8 us
    all_to_all x1, waiting for transfers between devices, local(): lax.all_to_all(served.reshape(local_feats, peers, look_cap, width), 'dp',...  44 us
    psum x2, blocking collectives, local(): lax.psum(contract_last(direct_bias_term, up_factor_weight[layer]), 'mp')  34.5 us
    psum x2, blocking collectives, cross_down(): return lax.psum(contract_last(state, v_layer), 'mp').astype(jnp.bfloat16)  33.8 us
    psum x1, blocking collectives, local(): grad_small = lax.psum(jnp.stack(bias_grads + [head_grad]), 'dp')  33.2 us
    unnamed x42, local copies, waits for them, and re-layouts  25.8 us
    all_to_all x1, blocking collectives, local(): lax.all_to_all(wanted.reshape(local_feats, peers, look_cap), 'dp', split_...  11.2 us
  transfers between devices with their start and end apart: 5, of which 3 were waited for; matrix products, arithmetic and copies ran while one was open for 12% of the time, Pallas kernels for 0%

commit v1 on v0

--- a/solution.py
+++ b/solution.py
@@ -1,6 +1,10 @@
+import functools
+
 import jax
 import jax.numpy as jnp
 from jax import lax
+from jax.experimental import pallas as pl
+from jax.experimental.pallas import tpu as pltpu
 from jax.sharding import PartitionSpec as P
 
 learn_rate = 0.5
@@ -174,9 +178,560 @@
     return (new_table, new_accum, grad_u, grad_v, grad_small, grad_pooled)
 
 
+F32, BF16 = jnp.float32, jnp.bfloat16
+MESH = pl.DeviceIdType.MESH
+
+
+def one_hot_rows(count, first, row):
+    spots = lax.broadcasted_iota(jnp.int32, (count, row.shape[1]), 0) + first
+    return jnp.where(spots == row, 1.0, 0.0).astype(BF16)
+
+
+def fused_kernel(
+    batch_total,
+    table_ref,
+    accum_ref,
+    stale_ref,
+    gown_ref,
+    grow_ref,
+    lown_ref,
+    lrow_ref,
+    len_ref,
+    label_ref,
+    u_ref,
+    v_ref,
+    bias_ref,
+    head_ref,
+    new_table_ref,
+    new_accum_ref,
+    gu_ref,
+    gv_ref,
+    small_ref,
+    pooled_ref,
+    meta_tx,
+    meta_rx,
+    srv_tx,
+    srv_rx,
+    g_tx,
+    g_rx,
+    pool_acc,
+    start,
+    st1,
+    st2,
+    cr,
+    up2,
+    up1,
+    db,
+    dn,
+    bk,
+    tx1,
+    rx1,
+    tx2,
+    rx2,
+    ltx,
+    lrx,
+    slope_s,
+    small_tx,
+    small_rx,
+    x_tx,
+    x_rx,
+    own,
+    z_tx,
+    z_rx,
+    meta_ss,
+    meta_rs,
+    srv_ss,
+    srv_rs,
+    g_ss,
+    g_rs,
+    ar_ss,
+    ar_rs,
+    l_ss,
+    l_rs,
+    small_ss,
+    small_rs,
+    x_ss,
+    x_rs,
+    z_ss,
+    z_rs,
+):
+    d = lax.axis_index("dp")
+    m = lax.axis_index("mp")
+    peers = meta_tx.shape[0]
+    feats, rows, width = table_ref.shape
+    count = gown_ref.shape[1]
+    cap = meta_tx.shape[2]
+    batch, cols = start.shape
+    half = batch // 2
+    chunk = 256
+    x = lax.rem(d, 2)
+    z = d // 2
+    core = lax.rem(m, 2)
+    nz = peers // 2
+
+    def dp_peer(i):
+        return {"dp": lax.rem(d + i, peers)}
+
+    def z_peer(i):
+        return {"dp": lax.rem(z + i, nz) * 2 + x}
+
+    def remote(src, dst, ss, rs, dev):
+        return pltpu.make_async_remote_copy(
+            src_ref=src, dst_ref=dst, send_sem=ss, recv_sem=rs, device_id=dev, device_id_type=MESH
+        )
+
+    barrier = pltpu.get_barrier_semaphore()
+    for i in range(1, peers):
+        pl.semaphore_signal(barrier, inc=1, device_id=dp_peer(i), device_id_type=MESH)
+    for i in range(1, 4):
+        pl.semaphore_signal(
+            barrier, inc=1, device_id={"mp": lax.rem(m + i, 4)}, device_id_type=MESH
+        )
+
+    peer_col = lax.broadcasted_iota(jnp.int32, (peers, count), 0)
+    earlier = jnp.where(
+        lax.broadcasted_iota(jnp.int32, (count, count), 0)
+        < lax.broadcasted_iota(jnp.int32, (count, count), 1),
+        1.0,
+        0.0,
+    ).astype(BF16)
+
+    def order_of(owner):
+        hot = jnp.where(peer_col == owner, 1.0, 0.0)
+        before = jnp.dot(hot.astype(BF16), earlier, preferred_element_type=F32)
+        return jnp.sum(before * hot, axis=0, keepdims=True)
+
+    g_slots, l_slots, l_orders = [], [], []
+    for f in range(feats):
+        go, lo = gown_ref[f : f + 1, :], lown_ref[f : f + 1, :]
+        g_slots.append(go * cap + order_of(go).astype(jnp.int32))
+        l_orders.append(order_of(lo))
+        l_slots.append(lo * cap + l_orders[-1].astype(jnp.int32))
+
+    def split_row(row):
+        hi = row // 256
+        return [hi.astype(F32), (row - hi * 256).astype(F32)]
+
+    pad = jnp.zeros((6, count), F32)
+
+    def make_meta(p, _):
+        for f in range(feats):
+            for spot, slots, ref in ((f, l_slots[f], lrow_ref), (feats + f, g_slots[f], grow_ref)):
+                hot = one_hot_rows(cap, p * cap, slots)
+                vals = jnp.concatenate(split_row(ref[f : f + 1, :]) + [pad], axis=0).astype(BF16)
+                res = lax.dot_general(
+                    vals, hot, (((1,), (1,)), ((), ())), preferred_element_type=F32
+                )
+                meta_tx[p, spot : spot + 1, :] = (res[0:1] * 256.0 + res[1:2]).astype(jnp.int32)
+        return 0
+
+    lax.fori_loop(0, peers, make_meta, 0)
+    pl.semaphore_wait(barrier, peers - 1 + 3)
+
+    def meta_copy(i):
+        return remote(
+            meta_tx.at[lax.rem(d + i, peers)], meta_rx.at[i], meta_ss.at[i], meta_rs.at[i], dp_peer(i)
+        )
+
+    def srv_copy(i):
+        return remote(srv_tx.at[i], srv_rx.at[i], srv_ss.at[i], srv_rs.at[i], dp_peer(peers - i))
+
+    def g_copy(i):
+        return remote(g_tx.at[i], g_rx.at[i], g_ss.at[i], g_rs.at[i], dp_peer(i))
+
+    def loop_peers(body):
+        def step(i, _):
+            body(i)
+            return 0
+
+        lax.fori_loop(1, peers, step, 0)
+
+    loop_peers(lambda i: meta_copy(i).start())
+    meta_rx[0] = meta_tx[d]
+
+    def pack(i, dst):
+        p = lax.rem(d + i, peers)
+        for f in range(feats):
+            dst[i, f] = jnp.dot(
+                one_hot_rows(cap, p * cap, g_slots[f]), stale_ref[f], preferred_element_type=F32
+            ).astype(BF16)
+
+    pack(0, g_rx)
+    loop_peers(lambda i: pack(i, g_tx))
+
+    def serve(i, dst):
+        for f in range(feats):
+            hot = one_hot_rows(rows, 0, meta_rx[i, f : f + 1, :])
+            dst[i, f] = lax.dot_general(
+                hot,
+                table_ref[f].astype(BF16),
+                (((0,), (0,)), ((), ())),
+                preferred_element_type=F32,
+            ).astype(BF16)
+
+    def serve_peer(i):
+        meta_copy(i).wait_recv()
+        serve(i, srv_tx)
+        srv_copy(i).start()
+
+    loop_peers(serve_peer)
+    serve(0, srv_rx)
+
+    packed = jnp.concatenate(
+        [lown_ref[f : f + 1, :].astype(F32) for f in range(feats)] + l_orders, axis=0
+    ).astype(BF16)
+    bag = count // batch
+    pick_n = lax.broadcasted_iota(jnp.int32, (count, batch), 0)
+    pick_b = lax.broadcasted_iota(jnp.int32, (count, batch), 1)
+    member_slots = []
+    for k in range(bag):
+        pick = jnp.where(pick_n == pick_b * bag + k, 1.0, 0.0).astype(BF16)
+        got = jnp.dot(packed, pick, preferred_element_type=F32)
+        slot = (got[:feats] * float(cap) + got[feats:]).astype(jnp.int32)
+        member_slots.append(jnp.where(len_ref[...] > k, slot, -1))
+
+    def pool(i):
+        p = lax.rem(d + i, peers)
+        spots = lax.broadcasted_iota(jnp.int32, (cap, batch), 0) + p * cap
+        for f in range(feats):
+            mix = jnp.zeros((cap, batch), F32)
+            for k in range(bag):
+                mix = mix + jnp.where(spots == member_slots[k][f : f + 1, :], 1.0, 0.0)
+            part = lax.dot_general(
+                mix.astype(BF16),
+                srv_rx[i, f],
+                (((0,), (0,)), ((), ())),
+                preferred_element_type=F32,
+            )
+            pool_acc[:, f * width : (f + 1) * width] += part
+
+    pool_acc[...] = jnp.zeros_like(pool_acc)
+    pool(0)
+
+    def pool_peer(i):
+        srv_copy(i).wait_recv()
+        pool(i)
+
+    loop_peers(pool_peer)
+    loop_peers(lambda i: g_copy(i).start())
+    start[...] = pool_acc[...].astype(BF16)
+
+    mine = pl.ds(pl.multiple_of(core * half, half), half)
+    other = pl.ds(pl.multiple_of((1 - core) * half, half), half)
+    core_peer = {"mp": m + 1 - 2 * core}
+    y_peer = {"mp": lax.rem(m + 2, 4)}
+
+    def reduce_mp(r, left, right, dst, beside):
+        nt = (((1,), (1,)), ((), ()))
+        tx1[r] = lax.dot_general(left[other, :], right, nt, preferred_element_type=F32).astype(BF16)
+        one = remote(tx1.at[r], rx1.at[r], ar_ss.at[r, 0], ar_rs.at[r, 0], core_peer)
+        one.start()
+        part = lax.dot_general(left[mine, :], right, nt, preferred_element_type=F32)
+        one.wait_recv()
+        tx2[r] = (part + rx1[r].astype(F32)).astype(BF16)
+        two = remote(tx2.at[r], rx2.at[r], ar_ss.at[r, 1], ar_rs.at[r, 1], y_peer)
+        two.start()
+        beside()
+        two.wait_recv()
+        dst[mine, :] = (tx2[r].astype(F32) + rx2[r].astype(F32)).astype(BF16)
+        three = remote(dst.at[mine, :], dst.at[mine, :], ar_ss.at[r, 2], ar_rs.at[r, 2], core_peer)
+        three.start()
+        three.wait_recv()
+        one.wait_send()
+        two.wait_send()
+        three.wait_send()
+
+    def loop_chunks(body):
+        def step(j, _):
+            body(pl.ds(pl.multiple_of(j * chunk, chunk), chunk))
+            return 0
+
+        lax.fori_loop(0, cols // chunk, step, 0)
+
+    states = [start, st1, st2]
+    slope_s[...] = jnp.zeros_like(slope_s)
+    for layer in range(2):
+        reduce_mp(layer, states[layer], v_ref[layer], dn.at[layer], lambda: None)
+
+        def forward(at, layer=layer):
+            cross = (
+                jnp.dot(dn[layer], u_ref[layer, :, at], preferred_element_type=F32)
+                + bias_ref[layer : layer + 1, at]
+            )
+            cr[layer, :, at] = cross
+            nxt = start[:, at].astype(F32) * cross + states[layer][:, at].astype(F32)
+            states[layer + 1][:, at] = nxt.astype(BF16)
+            if layer == 1:
+                term = nxt.astype(BF16).astype(F32) * head_ref[:, at]
+                slope_s[...] += term[:, 0:128] + term[:, 128:256]
+
+        loop_chunks(forward)
+
+    column = jnp.sum(slope_s[...], axis=1, keepdims=True)
+    wide = jnp.transpose(jnp.broadcast_to(column, (batch, 128)))
+    ltx[...] = wide[0:8, :]
+    logit_copies = [
+        remote(ltx, lrx.at[i], l_ss.at[i], l_rs.at[i], {"mp": lax.rem(m + i, 4)})
+        for i in range(1, 4)
+    ]
+    for copy in logit_copies:
+        copy.start()
+    for copy in logit_copies:
+        copy.wait_recv()
+    logit = ltx[0:1, :] + lrx[1, 0:1, :] + lrx[2, 0:1, :] + lrx[3, 0:1, :]
+    slope_row = (jax.nn.sigmoid(logit) - label_ref[...].astype(F32)) / jnp.sqrt(F32(batch_total))
+    slope_s[...] = jnp.transpose(jnp.broadcast_to(slope_row, (128, batch)))
+
+    block = gu_ref.shape[1]
+
+    def x_copy(q):
+        return remote(x_tx.at[q], x_rx.at[q], x_ss.at[q], x_rs.at[q], {"dp": d + 1 - 2 * x})
+
+    def z_copy(q, i):
+        return remote(
+            z_tx.at[q, lax.rem(z + i, nz)],
+            z_rx.at[q, i - 1],
+            z_ss.at[q, i - 1],
+            z_rs.at[q, i - 1],
+            z_peer(i),
+        )
+
+    def factor(q, left, right):
+        def step(j, _):
+            at = pl.ds(pl.multiple_of(j * 2 * block, 2 * block), 2 * block)
+            res = lax.dot_general(
+                left[:, at], right[...], (((0,), (0,)), ((), ())), preferred_element_type=F32
+            )
+            lower, upper = res[:block], res[block:]
+            own[q, j] = jnp.where(x == 0, lower, upper)
+            x_tx[q, j] = jnp.where(x == 0, upper, lower).astype(BF16)
+            return 0
+
+        lax.fori_loop(0, nz, step, 0)
+        x_copy(q).start()
+
+    def merge(q):
+        x_copy(q).wait_recv()
+
+        def step(j, _):
+            total = own[q, j] + x_rx[q, j].astype(F32)
+            own[q, j] = total
+            z_tx[q, j] = total.astype(BF16)
+            return 0
+
+        lax.fori_loop(0, nz, step, 0)
+        for i in range(1, nz):
+            z_copy(q, i).start()
+
+    def finish(q, out, layer):
+        for i in range(1, nz):
+            z_copy(q, i).wait_recv()
+        total = own[q, z]
+        for i in range(1, nz):
+            total = total + z_rx[q, i - 1].astype(F32)
+        out[layer] = total
+
+    small_tx[...] = jnp.zeros_like(small_tx)
+
+    def top(at):
+        slope = slope_s[:, 0:1]
+        up = slope * head_ref[:, at]
+        direct = up * start[:, at].astype(F32)
+        up2[:, at] = up
+        db[1, :, at] = direct.astype(BF16)
+        small_tx[1:2, at] = jnp.sum(direct, axis=0, keepdims=True)
+        small_tx[2:3, at] = jnp.sum(slope * st2[:, at].astype(F32), axis=0, keepdims=True)
+
+    loop_chunks(top)
+    reduce_mp(2, db.at[1], u_ref[1], bk.at[1], lambda: factor(0, dn.at[1], db.at[1]))
+
+    def middle(at):
+        up = up2[:, at] + jnp.dot(bk[1], v_ref[1, :, at], preferred_element_type=F32)
+        direct = up * start[:, at].astype(F32)
+        up1[:, at] = up
+        db[0, :, at] = direct.astype(BF16)
+        small_tx[0:1, at] = jnp.sum(direct, axis=0, keepdims=True)
+
+    loop_chunks(middle)
+
+    def small_copy(i):
+        return remote(small_tx, small_rx.at[i], small_ss.at[i], small_rs.at[i], dp_peer(i))
+
+    def beside_last():
+        factor(1, bk.at[1], st1)
+        factor(2, dn.at[0], db.at[0])
+        merge(0)
+
+    reduce_mp(3, db.at[0], u_ref[0], bk.at[0], beside_last)
+    factor(3, bk.at[0], start)
+    loop_peers(lambda i: small_copy(i).start())
+    merge(1)
+
+    def bottom(at):
+        up = up1[:, at] + jnp.dot(bk[0], v_ref[0, :, at], preferred_element_type=F32)
+        pooled_ref[:, at] = (
+            up + (up2[:, at] * cr[1, :, at] + up1[:, at] * cr[0, :, at])
+        ).astype(BF16)
+
+    loop_chunks(bottom)
+    merge(2)
+    merge(3)
+
+    loop_peers(lambda i: g_copy(i).wait_recv())
+
+    def update(f, _):
+        def add(i, total):
+            hot = one_hot_rows(rows, 0, meta_rx[i, pl.ds(feats + f, 1), :])
+            return total + jnp.dot(hot, g_rx[i, f], preferred_element_type=F32)
+
+        summed = lax.fori_loop(0, peers, add, jnp.zeros((rows, width), F32))
+        mean = jnp.sum(summed * summed, axis=1, keepdims=True) * (1.0 / width)
+        before = jnp.transpose(jnp.broadcast_to(accum_ref[pl.ds(f, 1), :], (128, rows)))[:, 0:1]
+        fresh = before + mean
+        new_accum_ref[pl.ds(f, 1), :] = jnp.transpose(jnp.broadcast_to(fresh, (rows, 128)))[0:1, :]
+        new_table_ref[f] = table_ref[f] - summed * (learn_rate / jnp.sqrt(fresh))
+        return 0
+
+    lax.fori_loop(0, feats, update, 0)
+
+    loop_peers(lambda i: small_copy(i).wait_recv())
+    total = small_tx[...]
+    for i in range(1, peers):
+        total = total + small_rx[i]
+    small_ref[...] = total
+    finish(0, gu_ref, 1)
+    finish(1, gv_ref, 1)
+    finish(2, gu_ref, 0)
+    finish(3, gv_ref, 0)
+
+    def drain(i):
+        meta_copy(i).wait_send()
+        srv_copy(i).wait_send()
+        g_copy(i).wait_send()
+        small_copy(i).wait_send()
+
+    loop_peers(drain)
+    for copy in logit_copies:
+        copy.wait_send()
+    for q in range(4):
+        x_copy(q).wait_send()
+        for i in range(1, nz):
+            z_copy(q, i).wait_send()
+
+
+def fused_local(
+    embed_table,
+    accum,
+    stale_grad,
+    grad_owner,
+    grad_row,
+    lookup_owner,
+    lookup_row,
+    bag_len,
+    label,
+    up_factor_weight,
+    v_weight,
+    cross_bias,
+    head_weight,
+):
+    peers = lax.axis_size("dp")
+    feats, rows, width = embed_table.shape
+    count = stale_grad.shape[1]
+    cap = 2 * count // peers
+    batch = bag_len.shape[1]
+    layers, rank, cols = v_weight.shape
+    block = rank // peers
+    half = batch // 2
+    nz = peers // 2
+    dma = pltpu.SemaphoreType.DMA
+    vmem = pl.BlockSpec(memory_space=pltpu.VMEM)
+    shape = jax.ShapeDtypeStruct
+    outs = pl.pallas_call(
+        functools.partial(fused_kernel, batch * peers),
+        out_shape=[
+            shape((feats, rows, width), F32),
+            shape((feats, rows), F32),
+            shape((layers, block, cols), F32),
+            shape((layers, block, cols), F32),
+            shape((8, cols), F32),
+            shape((batch, cols), BF16),
+        ],
+        in_specs=[vmem] * 13,
+        out_specs=[vmem] * 6,
+        scratch_shapes=[
+            pltpu.VMEM((peers, 2 * feats, cap), jnp.int32),
+            pltpu.VMEM((peers, 2 * feats, cap), jnp.int32),
+            pltpu.VMEM((peers, feats, cap, width), BF16),
+            pltpu.VMEM((peers, feats, cap, width), BF16),
+            pltpu.VMEM((peers, feats, cap, width), BF16),
+            pltpu.VMEM((peers, feats, cap, width), BF16),
+            pltpu.VMEM((batch, cols), F32),
+            pltpu.VMEM((batch, cols), BF16),
+            pltpu.VMEM((batch, cols), BF16),
+            pltpu.VMEM((batch, cols), BF16),
+            pltpu.VMEM((2, batch, cols), F32),
+            pltpu.VMEM((batch, cols), F32),
+            pltpu.VMEM((batch, cols), F32),
+            pltpu.VMEM((2, batch, cols), BF16),
+            pltpu.VMEM((2, batch, rank), BF16),
+            pltpu.VMEM((2, batch, rank), BF16),
+            pltpu.VMEM((4, half, rank), BF16),
+            pltpu.VMEM((4, half, rank), BF16),
+            pltpu.VMEM((4, half, rank), BF16),
+            pltpu.VMEM((4, half, rank), BF16),
+            pltpu.VMEM((8, batch), F32),
+            pltpu.VMEM((4, 8, batch), F32),
+            pltpu.VMEM((batch, 128), F32),
+            pltpu.VMEM((8, cols), F32),
+            pltpu.VMEM((peers, 8, cols), F32),
+            pltpu.VMEM((4, nz, block, cols), BF16),
+            pltpu.VMEM((4, nz, block, cols), BF16),
+            pltpu.VMEM((4, nz, block, cols), F32),
+            pltpu.VMEM((4, nz, block, cols), BF16),
+            pltpu.VMEM((4, nz - 1, block, cols), BF16),
+            dma((peers,)),
+            dma((peers,)),
+            dma((peers,)),
+            dma((peers,)),
+            dma((peers,)),
+            dma((peers,)),
+            dma((4, 3)),
+            dma((4, 3)),
+            dma((4,)),
+            dma((4,)),
+            dma((peers,)),
+            dma((peers,)),
+            dma((4,)),
+            dma((4,)),
+            dma((4, nz - 1)),
+            dma((4, nz - 1)),
+        ],
+        compiler_params=pltpu.CompilerParams(
+            collective_id=0, has_side_effects=True, vmem_limit_bytes=60 * 1024 * 1024
+        ),
+    )(
+        embed_table,
+        accum,
+        stale_grad,
+        grad_owner[:, :, 0],
+        grad_row,
+        lookup_owner[:, :, 0],
+        lookup_row,
+        bag_len,
+        label.reshape(1, batch),
+        up_factor_weight,
+        v_weight,
+        cross_bias,
+        head_weight.reshape(1, cols),
+    )
+    new_table, new_accum, grad_u, grad_v, grad_small, grad_pooled = outs
+    return new_table, new_accum, grad_u, grad_v, grad_small[:3], grad_pooled
+
+
 def solution(mesh):
+    fits = mesh.shape["dp"] == 8 and mesh.shape["mp"] == 4
     return jax.shard_map(
-        local,
+        fused_local if fits else local,
         mesh=mesh,
         in_specs=(
             P("mp", "dp", None),

time: 392 us -> 180 us (0.46)
  Pallas kernels: 0 us -> 170 us
  waiting for transfers between devices: 150 us -> 0 us
  blocking collectives: 118 us -> 0 us
  local copies, waits for them, and re-layouts: 46.2 us -> 8.81 us
  matrix products: 32.4 us -> 0 us
  starting transfers between devices: 14.7 us -> 0 us
  between operations: 14.4 us -> 0.65 us
  other arithmetic: 12.8 us -> 0 us
    pallas_call x0 -> x1, Pallas kernels: none -> 170 us  [fused_local(): pl.pallas_call(functools.partial(fused_kernel, batch * peers), out_shape=...]
    psum x6 -> x0, blocking collectives: 107 us -> none  [the longest x2 34.5 us: local(): lax.psum(contract_last(direct_bias_term, up_factor_weight[layer]), 'mp')]
    all_to_all x3 -> x0, waiting for transfers between devices: 90.8 us -> none  [the longest x1 46.8 us: local(): lax.all_to_all(send_grads.reshape(local_feats, peers, grad_cap, width), '...]
    reduce_scatter x2 -> x0, waiting for transfers between devices: 59.4 us -> none  [the longest x1 59.4 us: local(): lax.psum_scatter(grad_v, 'dp', scatter_dimension=1, tiled=True)]
    dot_general x18 -> x0, matrix products: 32.4 us -> none  [the longest x4 5.95 us: contract_last(): lax.dot_general(left, right, (((1,), (1,)), ((), ())), preferred_element_...]
    unnamed x42 -> x14, local copies, waits for them, and re-layouts: 25.8 us -> 7.45 us
    all_to_all x3 -> x0, starting transfers between devices: 14.7 us -> none  [the longest x1 5.38 us: local(): lax.all_to_all(send_grads.reshape(local_feats, peers, grad_cap, width), '...]
    reshape x7 -> x0, local copies, waits for them, and re-layouts: 12.1 us -> none  [the longest x1 4.2 us: local(): recv_grads.reshape(local_feats, grad_total, width)]
  transfers between devices with their start and end apart: 5 -> 0, of which waited for: 3 -> 0; matrix products, arithmetic and copies ran while one was open for 12% -> 0% of each run, Pallas kernels for 0% -> 0%
where the time goes in v1:
time: 180 us
  Pallas kernels  170 us (94%)
  local copies, waits for them, and re-layouts  8.81 us (5%)
    pallas_call x1, Pallas kernels, fused_local(): pl.pallas_call(functools.partial(fused_kernel, batch * peers), out_shape=...  170 us
    unnamed x14, local copies, waits for them, and re-layouts  7.45 us

profile of v1, /device:TPU:2, one launch (start us, length us, event | category | flops | bytes accessed | tf_op | source)
XLA Modules:
  0.0 179.7 jit_solution(16252373803847433817)
XLA Ops:
  0.6 1.3 copy_bitcast_fusion
  2.0 170.2 %shard_map.172 = (f32[4,512,256]{2,1,0:T(8,128)}, f32[4,512]{1,0:T(4,128)}, f32[2,64,1024]{2,1,0:T(8,128)}, f32[2,64,1024]{2,1,0:T(8,128)}, f32[8,1024]{1,0:T(8,128)}, /*index=5*/bf16[256,1024]{1,0:T(8,128)(2,1)}) custom-call(f32[4,512,256]{2,1,0:T(8,128)} %table_ref.1, f32[4,512]{1,0:T(4,128)} %accum_ref.1, bf16[4,512,256]{2,1,0:T(8,128)(2,1)} %stale_ref.1, ...), custom_call_target="tpu_custom_call" | custom-call | tf_op jit(solution)/shard_map/pallas_call | solution.py:649
  172.2 1.4 slice.3
  173.6 0.0 copy-start.3
  173.6 0.0 copy-start.2
  173.6 0.0 copy-start.1
  173.6 3.1 %copy.28 = f32[4,512,256]{2,1,0:T(8,128)} copy(f32[4,512,256]{2,1,0:T(8,128)} %get-tuple-element.26) | data formatting | bytes 4194304
  176.7 0.0 copy-done.3
  176.7 0.0 copy-start
  176.7 0.6 copy.29
  177.3 0.0 copy-done.2
  177.3 0.8 copy.30
  178.1 0.0 copy-done.1
  178.1 0.8 copy.31
  178.9 0.0 copy-done
  178.9 0.8 copy.32
Async XLA Ops:
  173.6 3.1 %copy-start.3 = (f32[4,512]{1,0:T(4,128)S(1)}, f32[4,512]{1,0:T(4,128)}, u32[]{:S(2)}) copy-start(f32[4,512]{1,0:T(4,128)} %get-tuple-element.27) | copy-start | bytes 24580
  173.6 3.7 %copy-start.2 = (f32[2,64,1024]{2,1,0:T(8,128)S(1)}, f32[2,64,1024]{2,1,0:T(8,128)}, u32[]{:S(2)}) copy-start(f32[2,64,1024]{2,1,0:T(8,128)} %get-tuple-element.28) | copy-start | bytes 1572868
  173.6 4.5 %copy-start.1 = (f32[2,64,1024]{2,1,0:T(8,128)S(1)}, f32[2,64,1024]{2,1,0:T(8,128)}, u32[]{:S(2)}) copy-start(f32[2,64,1024]{2,1,0:T(8,128)} %get-tuple-element.29) | copy-start | bytes 1572868
  176.7 2.2 %copy-start = (bf16[256,1024]{1,0:T(8,128)(2,1)S(1)}, bf16[256,1024]{1,0:T(8,128)(2,1)}, u32[]{:S(2)}) copy-start(bf16[256,1024]{1,0:T(8,128)(2,1)} %get-tuple-element.31) | copy-start | bytes 1572868

commit v2 on v1

--- a/solution.py
+++ b/solution.py
@@ -210,6 +210,9 @@
     pooled_ref,
     meta_tx,
     meta_rx,
+    gmeta_tx,
+    gmeta_rx,
+    table_s,
     srv_tx,
     srv_rx,
     g_tx,
@@ -240,6 +243,8 @@
     z_rx,
     meta_ss,
     meta_rs,
+    gmeta_ss,
+    gmeta_rs,
     srv_ss,
     srv_rs,
     g_ss,
@@ -303,8 +308,7 @@
 
     g_slots, l_slots, l_orders = [], [], []
     for f in range(feats):
-        go, lo = gown_ref[f : f + 1, :], lown_ref[f : f + 1, :]
-        g_slots.append(go * cap + order_of(go).astype(jnp.int32))
+        lo = lown_ref[f : f + 1, :]
         l_orders.append(order_of(lo))
         l_slots.append(lo * cap + l_orders[-1].astype(jnp.int32))
 
@@ -314,30 +318,33 @@
 
     pad = jnp.zeros((6, count), F32)
 
-    def make_meta(p, _):
+    def rows_in_slots(ref, f, hot):
+        vals = jnp.concatenate(split_row(ref[f : f + 1, :]) + [pad], axis=0).astype(BF16)
+        res = lax.dot_general(vals, hot, (((1,), (1,)), ((), ())), preferred_element_type=F32)
+        return (res[0:1] * 256.0 + res[1:2]).astype(jnp.int32)
+
+    def g_copy(i):
+        return remote(g_tx.at[i], g_rx.at[i], g_ss.at[i], g_rs.at[i], dp_peer(i))
+
+    def send_grads(first, last):
+        for i in range(first, last):
+            gmeta_copy(i).start()
+            g_copy(i).start()
+
+    def ask(i, dst):
+        p = lax.rem(d + i, peers)
         for f in range(feats):
-            for spot, slots, ref in ((f, l_slots[f], lrow_ref), (feats + f, g_slots[f], grow_ref)):
-                hot = one_hot_rows(cap, p * cap, slots)
-                vals = jnp.concatenate(split_row(ref[f : f + 1, :]) + [pad], axis=0).astype(BF16)
-                res = lax.dot_general(
-                    vals, hot, (((1,), (1,)), ((), ())), preferred_element_type=F32
-                )
-                meta_tx[p, spot : spot + 1, :] = (res[0:1] * 256.0 + res[1:2]).astype(jnp.int32)
-        return 0
-
-    lax.fori_loop(0, peers, make_meta, 0)
-    pl.semaphore_wait(barrier, peers - 1 + 3)
+            hot = one_hot_rows(cap, p * cap, l_slots[f])
+            dst[i, f : f + 1, :] = rows_in_slots(lrow_ref, f, hot)
 
     def meta_copy(i):
-        return remote(
-            meta_tx.at[lax.rem(d + i, peers)], meta_rx.at[i], meta_ss.at[i], meta_rs.at[i], dp_peer(i)
-        )
+        return remote(meta_tx.at[i], meta_rx.at[i], meta_ss.at[i], meta_rs.at[i], dp_peer(i))
+
+    def gmeta_copy(i):
+        return remote(gmeta_tx.at[i], gmeta_rx.at[i], gmeta_ss.at[i], gmeta_rs.at[i], dp_peer(i))
 
     def srv_copy(i):
         return remote(srv_tx.at[i], srv_rx.at[i], srv_ss.at[i], srv_rs.at[i], dp_peer(peers - i))
-
-    def g_copy(i):
-        return remote(g_tx.at[i], g_rx.at[i], g_ss.at[i], g_rs.at[i], dp_peer(i))
 
     def loop_peers(body):
         def step(i, _):
@@ -346,25 +353,23 @@
 
         lax.fori_loop(1, peers, step, 0)
 
-    loop_peers(lambda i: meta_copy(i).start())
-    meta_rx[0] = meta_tx[d]
-
-    def pack(i, dst):
-        p = lax.rem(d + i, peers)
-        for f in range(feats):
-            dst[i, f] = jnp.dot(
-                one_hot_rows(cap, p * cap, g_slots[f]), stale_ref[f], preferred_element_type=F32
-            ).astype(BF16)
-
-    pack(0, g_rx)
-    loop_peers(lambda i: pack(i, g_tx))
+    pl.semaphore_wait(barrier, peers - 1 + 3)
+
+    def ask_peer(i):
+        ask(i, meta_tx)
+        meta_copy(i).start()
+
+    loop_peers(ask_peer)
+    ask(0, meta_rx)
+    for f in range(feats):
+        table_s[f] = table_ref[f].astype(BF16)
 
     def serve(i, dst):
         for f in range(feats):
             hot = one_hot_rows(rows, 0, meta_rx[i, f : f + 1, :])
             dst[i, f] = lax.dot_general(
                 hot,
-                table_ref[f].astype(BF16),
+                table_s[f],
                 (((0,), (0,)), ((), ())),
                 preferred_element_type=F32,
             ).astype(BF16)
@@ -374,7 +379,29 @@
         serve(i, srv_tx)
         srv_copy(i).start()
 
+    for f in range(feats):
+        owner = gown_ref[f : f + 1, :]
+        g_slots.append(owner * cap + order_of(owner).astype(jnp.int32))
+
+    def pack(i, dst, ids):
+        p = lax.rem(d + i, peers)
+        for f in range(feats):
+            hot = one_hot_rows(cap, p * cap, g_slots[f])
+            dst[i, f] = jnp.dot(hot, stale_ref[f], preferred_element_type=F32).astype(BF16)
+            ids[i, f : f + 1, :] = rows_in_slots(grow_ref, f, hot)
+
+    for i in range(1, 3):
+        pack(i, g_tx, gmeta_tx)
+        send_grads(i, i + 1)
+
     loop_peers(serve_peer)
+
+    pack(0, g_rx, gmeta_rx)
+    def pack_peer(i, _):
+        pack(i, g_tx, gmeta_tx)
+        return 0
+
+    lax.fori_loop(3, peers, pack_peer, 0)
     serve(0, srv_rx)
 
     packed = jnp.concatenate(
@@ -413,7 +440,7 @@
         pool(i)
 
     loop_peers(pool_peer)
-    loop_peers(lambda i: g_copy(i).start())
+    send_grads(3, peers)
     start[...] = pool_acc[...].astype(BF16)
 
     mine = pl.ds(pl.multiple_of(core * half, half), half)
@@ -577,11 +604,15 @@
     merge(2)
     merge(3)
 
-    loop_peers(lambda i: g_copy(i).wait_recv())
+    def landed(i):
+        gmeta_copy(i).wait_recv()
+        g_copy(i).wait_recv()
+
+    loop_peers(landed)
 
     def update(f, _):
         def add(i, total):
-            hot = one_hot_rows(rows, 0, meta_rx[i, pl.ds(feats + f, 1), :])
+            hot = one_hot_rows(rows, 0, gmeta_rx[i, pl.ds(f, 1), :])
             return total + jnp.dot(hot, g_rx[i, f], preferred_element_type=F32)
 
         summed = lax.fori_loop(0, peers, add, jnp.zeros((rows, width), F32))
@@ -606,6 +637,7 @@
 
     def drain(i):
         meta_copy(i).wait_send()
+        gmeta_copy(i).wait_send()
         srv_copy(i).wait_send()
         g_copy(i).wait_send()
         small_copy(i).wait_send()
@@ -659,8 +691,11 @@
         in_specs=[vmem] * 13,
         out_specs=[vmem] * 6,
         scratch_shapes=[
-            pltpu.VMEM((peers, 2 * feats, cap), jnp.int32),
-            pltpu.VMEM((peers, 2 * feats, cap), jnp.int32),
+            pltpu.VMEM((peers, feats, cap), jnp.int32),
+            pltpu.VMEM((peers, feats, cap), jnp.int32),
+            pltpu.VMEM((peers, feats, cap), jnp.int32),
+            pltpu.VMEM((peers, feats, cap), jnp.int32),
+            pltpu.VMEM((feats, rows, width), BF16),
             pltpu.VMEM((peers, feats, cap, width), BF16),
             pltpu.VMEM((peers, feats, cap, width), BF16),
             pltpu.VMEM((peers, feats, cap, width), BF16),
@@ -689,6 +724,8 @@
             pltpu.VMEM((4, nz, block, cols), F32),
             pltpu.VMEM((4, nz, block, cols), BF16),
             pltpu.VMEM((4, nz - 1, block, cols), BF16),
+            dma((peers,)),
+            dma((peers,)),
             dma((peers,)),
             dma((peers,)),
             dma((peers,)),

time: 180 us -> 178 us (0.989)
  Pallas kernels: 170 us -> 168 us
    pallas_call x1, Pallas kernels: 170 us -> 168 us  [fused_local(): pl.pallas_call(functools.partial(fused_kernel, batch * peers), out_shape=...]
where the time goes in v2:
time: 178 us; the launch traced here: 177 us
  Pallas kernels  168 us (94%)
  local copies, waits for them, and re-layouts  8.81 us (5%)
    pallas_call x1, Pallas kernels, fused_local(): pl.pallas_call(functools.partial(fused_kernel, batch * peers), out_shape=...  168 us
    unnamed x14, local copies, waits for them, and re-layouts  7.45 us

profile of v2, /device:TPU:2, one launch (start us, length us, event | category | flops | bytes accessed | tf_op | source)
XLA Modules:
  0.0 177.5 jit_solution(3125222660003057973)
XLA Ops:
  0.6 1.3 copy_bitcast_fusion
  2.0 168.0 %shard_map.172 = (f32[4,512,256]{2,1,0:T(8,128)}, f32[4,512]{1,0:T(4,128)}, f32[2,64,1024]{2,1,0:T(8,128)}, f32[2,64,1024]{2,1,0:T(8,128)}, f32[8,1024]{1,0:T(8,128)}, /*index=5*/bf16[256,1024]{1,0:T(8,128)(2,1)}) custom-call(f32[4,512,256]{2,1,0:T(8,128)} %table_ref.1, f32[4,512]{1,0:T(4,128)} %accum_ref.1, bf16[4,512,256]{2,1,0:T(8,128)(2,1)} %stale_ref.1, ...), custom_call_target="tpu_custom_call" | custom-call | tf_op jit(solution)/shard_map/pallas_call | solution.py:681
  170.0 1.4 slice.3
  171.3 0.0 copy-start.3
  171.3 0.0 copy-start.2
  171.3 0.0 copy-start.1
  171.3 3.1 %copy.28 = f32[4,512,256]{2,1,0:T(8,128)} copy(f32[4,512,256]{2,1,0:T(8,128)} %get-tuple-element.26) | data formatting | bytes 4194304
  174.5 0.0 copy-done.3
  174.5 0.0 copy-start
  174.5 0.6 copy.29
  175.1 0.0 copy-done.2
  175.1 0.8 copy.30
  175.9 0.0 copy-done.1
  175.9 0.8 copy.31
  176.7 0.0 copy-done
  176.7 0.8 copy.32
Async XLA Ops:
  171.3 3.1 %copy-start.3 = (f32[4,512]{1,0:T(4,128)S(1)}, f32[4,512]{1,0:T(4,128)}, u32[]{:S(2)}) copy-start(f32[4,512]{1,0:T(4,128)} %get-tuple-element.27) | copy-start | bytes 24580
  171.3 3.7 %copy-start.2 = (f32[2,64,1024]{2,1,0:T(8,128)S(1)}, f32[2,64,1024]{2,1,0:T(8,128)}, u32[]{:S(2)}) copy-start(f32[2,64,1024]{2,1,0:T(8,128)} %get-tuple-element.28) | copy-start | bytes 1572868
  171.3 4.5 %copy-start.1 = (f32[2,64,1024]{2,1,0:T(8,128)S(1)}, f32[2,64,1024]{2,1,0:T(8,128)}, u32[]{:S(2)}) copy-start(f32[2,64,1024]{2,1,0:T(8,128)} %get-tuple-element.29) | copy-start | bytes 1572868
  174.5 2.2 %copy-start = (bf16[256,1024]{1,0:T(8,128)(2,1)S(1)}, bf16[256,1024]{1,0:T(8,128)(2,1)}, u32[]{:S(2)}) copy-start(bf16[256,1024]{1,0:T(8,128)(2,1)} %get-tuple-element.31) | copy-start | bytes 1572868
